TPU v7x, 256 devices: a whole 4x4x8 slice. The times are simulated.
256 devices in a mesh: dp: 32 (over x, z), vocab: 8 (over y, core).
Axes of the slice: x: 4, y: 4, z: 8, core: 2. Of those that a mesh axis runs over, the one named last changes fastest.
Arguments:
- hidden_states: bfloat16 [8192, 8192], P('dp', 'vocab'), may hold values from -100 to 100, as said below
- logits: bfloat16 [8192, 128256], P('dp', 'vocab'), may hold values from -20 to 260
- targets: int32 [8192], P('dp'), may hold values from 0 to 128255
- input_proj: bfloat16 [8192, 64], P('vocab'), may hold values from -0.0625 to 0.0625
- output_proj: bfloat16 [128256, 64], P('vocab'), may hold values from -6 to 6
- query_ids: int32 [64], replicated, may hold values from 0 to 63
Outputs:
- scores: float32 [64, 64], P('dp')
Inputs may be any that keep to these rules, and one draw needn't show every extreme that they name: `hidden_states`: hidden states of order one to ten.
All inputs are finite; a program needn't handle non-finite values.
Results may differ from a plain program's by a relative error of at most 0.0003.
Values may be sent and summed in bfloat16 or wider, within the bound.
A program may use at most 64 MiB of HBM per device.

v0:
```python
import jax
import jax.numpy as jnp
from jax import lax
from jax.sharding import PartitionSpec as P

SEQ = 128


def body(hidden_states, logits, targets, input_proj, output_proj, query_ids):
    tok_rows = logits.shape[0]
    vocab_width = logits.shape[1]
    examples_here = tok_rows // SEQ
    values = logits.astype(jnp.float32)
    narrow_max = jnp.max(logits, axis=1)
    row_max = lax.pmax(narrow_max, "vocab").astype(jnp.float32)
    exp_terms = jnp.exp(values - row_max[:, None])
    row_total = lax.psum(jnp.sum(exp_terms, axis=1), "vocab")
    first_column = lax.axis_index("vocab") * vocab_width
    columns = lax.broadcasted_iota(jnp.int32, values.shape, 1) + first_column
    hit = (columns == targets[:, None]).astype(jnp.float32)
    out_grad = (exp_terms / row_total[:, None] - hit).astype(jnp.bfloat16)
    out_part = jnp.dot(out_grad, output_proj, preferred_element_type=jnp.float32)
    in_part = jnp.dot(hidden_states, input_proj, preferred_element_type=jnp.float32)
    in_low, out_low = lax.psum((in_part, out_part), "vocab")
    in_blocks = in_low.reshape(examples_here, SEQ, in_low.shape[1])
    out_blocks = out_low.reshape(examples_here, SEQ, out_low.shape[1])
    example_grad = jnp.einsum(
        "esi,eso->eio", in_blocks, out_blocks, precision=lax.Precision.HIGHEST
    )
    gathered = lax.all_gather(example_grad, "dp", axis=0, tiled=True)
    chosen = jnp.take(gathered, query_ids, axis=0)
    dots = jnp.einsum("eio,qio->eq", example_grad, chosen, precision=lax.Precision.HIGHEST)
    self_sq = jnp.sum(example_grad * example_grad, axis=(1, 2))
    query_sq = jnp.sum(chosen * chosen, axis=(1, 2))
    return dots * lax.rsqrt(self_sq + 1e-06)[:, None] * lax.rsqrt(query_sq + 1e-06)[None, :]


def solution(mesh):
    return jax.shard_map(
        body,
        mesh=mesh,
        in_specs=(
            P("dp", "vocab"),
            P("dp", "vocab"),
            P("dp"),
            P("vocab", None),
            P("vocab", None),
            P(),
        ),
        out_specs=P("dp", None),
        check_vma=False,
    )
```

profile of v0, /device:TPU:1, one launch (start us, length us, event | category | flops | bytes accessed | tf_op | source)
XLA Modules:
  0.0 217.6 jit_solution(14005098327153474215)
XLA Ops:
  6.5 0.0 copy-start
  6.5 0.0 all-reduce.3.cloned.1.call-start
  6.5 0.0 copy-start.4
  6.5 6.6 %reduce_max.9 = bf16[256]{0:T(256)(128)(2,1)S(1)} reduce(bf16[256,16032]{0,1:T(8,128)(2,1)} %param.7, bf16[]{:T(256)} %constant.9.clone.1), dimensions={1}, to_apply=%region_1.0 | reduce | flops 4103936 | bytes 8208898 | tf_op jit(solution)/shard_map/reduce_max | solution.py:14
  13.2 15.0 %pmax.7 = bf16[256]{0:T(256)(128)(2,1)S(1)} all-reduce(bf16[256]{0:T(256)(128)(2,1)S(1)} %reduce_max.9), channel_id=1, replica_groups=mesh['dp'=32,'vocab'=8] {'vocab'}, use_global_device_ids=true, to_apply=%region_2.0 | all-reduce | flops 256 | bytes 1024 | tf_op jit(solution)/shard_map/pmax | solution.py:15
  28.2 6.5 %fusion = f32[256]{0:T(256)S(1)} fusion(bf16[256,16032]{0,1:T(8,128)(2,1)} %param.7, f32[256]{0:T(256)S(1)} %convert_element_type.13), kind=kLoop, calls=%fused_computation.3 | loop fusion | flops 12312320 | bytes 8210432 | tf_op jit(solution)/shard_map/reduce_sum | solution.py:17
  34.7 13.1 %psum.22 = f32[256]{0:T(256)S(1)} all-reduce(f32[256]{0:T(256)S(1)} %fusion), channel_id=1, replica_groups=mesh['dp'=32,'vocab'=8] {'vocab'}, use_global_device_ids=true, to_apply=%region_4.0 | all-reduce | flops 256 | bytes 2048 | tf_op jit(solution)/shard_map/psum | solution.py:17
  47.8 0.0 copy-done
  47.8 0.0 copy-done.4
  47.9 0.0 copy-start.2
  47.9 0.0 copy-start.3
  47.9 0.0 copy-start.5
  47.9 10.8 %fusion.4 = f32[8,2,8,128]{3,2,1,0:T(8,128)S(1)} fusion(bf16[16032,64]{0,1:T(8,128)(2,1)S(1)} %copy-done, bf16[256,16032]{0,1:T(8,128)(2,1)} %param.7, s32[256]{0:T(256)S(1)} %copy-done.4, f32[256]{0:T(256)S(1)} %psum.22, f32[256]{0:T(256)S(1)} %convert_element_type.13, s32[16032]{0:T(1024)S(1)} %iota_add_fusion), kind=kOutput, calls=%fused_computation.8 | convolution fusion | flops 554065920 | bytes 10393216 | tf_op jit(solution)/shard_map/dot_general | solution.py:22
  58.7 0.6 copy.29
  59.3 0.0 copy-done.2
  59.3 0.0 copy-done.3
  59.3 0.3 convolution_bitcast_fusion
  59.6 0.6 copy.30
  60.2 0.0 all-reduce.3.cloned.1.call-update
  60.2 0.0 all-gather.2.cloned.1.call-start
  60.3 62.9 %all-reduce.3.cloned.1.call-done = (f32[2,128,64]{1,2,0:T(8,128)}, f32[2,128,64]{1,2,0:T(8,128)}) async-done(((f32[2,128,64]{1,2,0:T(8,128)}, f32[2,128,64]{1,2,0:T(8,128)}), (f32[2,128,64]{1,2,0:T(8,128)}, f32[2,128,64]{1,2,0:T(8,128)})) %all-reduce.3.cloned.1.call-update) | async-done | bytes 131088 | tf_op jit(solution)/shard_map/psum | solution.py:24
  123.2 1.7 multiply_reduce_fusion.1
  124.9 0.0 copy-start.1
  124.9 0.0 all-gather.2.cloned.1.call-update
  125.0 0.0 copy-done.5
  125.0 76.3 %all-gather.2.cloned.1.call-done = f32[64,64,64]{2,1,0:T(8,128)} async-done(((f32[2,64,64]{2,1,0:T(8,128)}), f32[64,64,64]{2,1,0:T(8,128)}) %all-gather.2.cloned.1.call-update) | async-done | bytes 1048592 | tf_op jit(solution)/shard_map/all_gather | solution.py:30
  201.3 3.6 %gather_fusion = f32[64,64,64]{2,1,0:T(8,128)} fusion(f32[64,64,64]{2,1,0:T(8,128)} %all-gather.2.cloned.1.call-done, s32[1024]{0:T(1024)S(1)} %pad_clamp_fusion), kind=kCustom, calls=%fused_computation | custom fusion | bytes 2097408 | tf_op jit(solution)/shard_map/jit(_take)/gather | solution.py:31
  204.9 2.6 %multiply_reduce_fusion = (f32[64]{0:T(128)S(1)}, f32[64,64,64]{2,1,0:T(8,128)S(1)}) fusion(f32[64,64,64]{2,1,0:T(8,128)} %gather_fusion, pred[64]{0:T(512)(128)(4,1)S(1)} %compare_and_fusion), kind=kLoop, calls=%fused_computation.7 | loop fusion | flops 786368 | bytes 2097472 | tf_op jit(solution)/shard_map/reduce_sum | solution.py:34
  207.5 0.0 copy-done.1
  207.5 3.3 %fusion.11 = f32[2,64]{1,0:T(2,128)} fusion(f32[64,64,64]{2,1,0:T(8,128)S(1)} %get-tuple-element.8, f32[2,64,64]{2,1,0:T(8,128)S(1)} %copy-done.1, f32[64]{0:T(128)S(1)} %add_rsqrt_fusion, f32[2]{0:T(128)S(1)} %add_rsqrt_fusion.1), kind=kOutput, calls=%fused_computation.12 | convolution fusion | flops 6291712 | bytes 1082120 | tf_op jit(solution)/shard_map/eio,qio->eq/dot_general | solution.py:32
  (7 shorter events, 0.0 us)
Async XLA Ops:
  6.5 41.3 %copy-start = (bf16[16032,64]{0,1:T(8,128)(2,1)S(1)}, bf16[16032,64]{0,1:T(8,128)(2,1)}, u32[]{:S(2)}) copy-start(bf16[16032,64]{0,1:T(8,128)(2,1)} %param.10) | copy-start | bytes 6156292
  6.5 116.7 %all-reduce.3.cloned.1.call-start = ((), (), s32[]{:S(2)}) async-start(), calls=%async_computation.1 | async-start | bytes 262144 | tf_op jit(solution)/shard_map/psum | solution.py:24
  6.5 41.3 %copy-start.4 = (s32[256]{0:T(256)S(1)}, s32[256]{0:T(256)}, u32[]{:S(2)}) copy-start(s32[256]{0:T(256)} %param.8) | copy-start | bytes 3076
  47.9 11.5 %copy-start.2 = (bf16[256,1024]{1,0:T(8,128)(2,1)S(1)}, bf16[256,1024]{1,0:T(8,128)(2,1)}, u32[]{:S(2)}) copy-start(bf16[256,1024]{1,0:T(8,128)(2,1)} %param.6) | copy-start | bytes 1572868
  47.9 11.4 %copy-start.3 = (bf16[1024,64]{0,1:T(8,128)(2,1)S(1)}, bf16[1024,64]{0,1:T(8,128)(2,1)}, u32[]{:S(2)}) copy-start(bf16[1024,64]{0,1:T(8,128)(2,1)} %param.9) | copy-start | bytes 393220
  47.9 77.1 %copy-start.5 = (s32[64]{0:T(128)S(1)}, s32[64]{0:T(128)}, u32[]{:S(2)}) copy-start(s32[64]{0:T(128)} %param.11) | copy-start | bytes 772
  60.2 141.1 %all-gather.2.cloned.1.call-start = ((), (), s32[]{:S(2)}) async-start(), calls=%async_computation | async-start | bytes 2162688 | tf_op jit(solution)/shard_map/all_gather | solution.py:30
  124.9 82.5 %copy-start.1 = (f32[2,64,64]{2,1,0:T(8,128)S(1)}, f32[2,64,64]{2,1,0:T(8,128)}, u32[]{:S(2)}) copy-start(f32[2,64,64]{2,1,0:T(8,128)} %get-tuple-element.10) | copy-start | bytes 98308
Sparse Core Ops, SparseCore 0:
  60.4 62.7 all-reduce.2
  126.1 75.1 all-gather.1
where the time goes:
time: 221 us; the launch traced here: 218 us
  waiting for transfers between devices  139 us (63%)
  blocking collectives  28.1 us (13%)
  matrix products  16.1 us (7%)
  other arithmetic  15.8 us (7%)
  between operations  13.5 us (6%)
  local copies, waits for them, and re-layouts  4.84 us (2%)
    all_gather x1, waiting for transfers between devices, body(): gathered = lax.all_gather(example_grad, 'dp', axis=0, tiled=True)  76.3 us
    psum x1, waiting for transfers between devices, body(): in_low, out_low = lax.psum((in_part, out_part), 'vocab')  62.9 us
    pmax x1, blocking collectives, body(): row_max = lax.pmax(narrow_max, 'vocab').astype(jnp.float32)  15 us
    psum x1, blocking collectives, body(): row_total = lax.psum(jnp.sum(exp_terms, axis=1), 'vocab')  13.1 us
    dot_general x1, matrix products, body(): jnp.dot(out_grad, output_proj, preferred_element_type=jnp.float32)  10.8 us
    reduce_max x1, other arithmetic, body(): narrow_max = jnp.max(logits, axis=1)  6.62 us
    reduce_sum x1, other arithmetic, body(): row_total = lax.psum(jnp.sum(exp_terms, axis=1), 'vocab')  6.5 us
  transfers between devices with their start and end apart: 2, of which 2 were waited for; matrix products, arithmetic and copies ran while one was open for 0% of the time, Pallas kernels for 0%

commit v1 on v0

v1 whole, which is shorter than its diff:
```python
import functools

import jax
import jax.numpy as jnp
from jax import lax
from jax.experimental import pallas as pl
from jax.experimental.pallas import tpu as pltpu
from jax.sharding import PartitionSpec as P

MESH = pl.DeviceIdType.MESH
F32 = jnp.float32
BF16 = jnp.bfloat16
SEQ = 128
LOG2E = 1.4426950408889634
HIGH = lax.Precision.HIGHEST
CHUNK = 2048
STEP = 256


def dot_t(a, b, precision=None):
    return lax.dot_general(
        a, b, (((1,), (1,)), ((), ())), precision=precision, preferred_element_type=F32
    )


def kernel(
    n_dp,
    n_voc,
    logits_hbm,
    proj_hbm,
    hidden_hbm,
    inproj_hbm,
    targets_ref,
    query_ref,
    out_ref,
    lbuf,
    ebuf,
    pbuf,
    hbuf,
    ibuf,
    in_part,
    in_parts,
    in_block,
    in_full,
    stat_src,
    stats,
    eg_src,
    eg_parts,
    slice_src,
    slices,
    sum_src,
    sums,
    load_sems,
    logit_sems,
    send_sems,
    recv_sems,
):
    rows, tokens = lbuf.shape
    me_d = lax.axis_index("dp")
    me_v = lax.axis_index("vocab")
    starts = list(range(0, rows, CHUNK))
    sizes = [min(CHUNK, rows - s) for s in starts]
    n_chunks = len(starts)

    loads = [
        pltpu.make_async_copy(hidden_hbm, hbuf, load_sems.at[0]),
        pltpu.make_async_copy(inproj_hbm, ibuf, load_sems.at[1]),
        pltpu.make_async_copy(proj_hbm, pbuf, load_sems.at[2]),
    ]
    chunk_loads = [
        pltpu.make_async_copy(
            logits_hbm.at[pl.ds(s, w)], lbuf.at[pl.ds(s, w)], logit_sems.at[c]
        )
        for c, (s, w) in enumerate(zip(starts, sizes))
    ]
    loads[0].start()
    loads[1].start()
    for copy in chunk_loads:
        copy.start()
    loads[2].start()

    def other_v(j):
        return lax.rem(me_v + j, n_voc)

    def other_d(j):
        return lax.rem(me_d + j, n_dp)

    barrier = pltpu.get_barrier_semaphore()

    def greet_v(j, carry):
        pl.semaphore_signal(
            barrier, inc=1, device_id=(me_d, other_v(j)), device_id_type=MESH
        )
        return carry

    def greet_d(j, carry):
        pl.semaphore_signal(
            barrier, inc=1, device_id=(other_d(j), me_v), device_id_type=MESH
        )
        return carry

    lax.fori_loop(1, n_voc, greet_v, 0)
    lax.fori_loop(1, n_dp, greet_d, 0)

    def send_v(src_of, dst, rnd):
        def one(j, carry):
            to = other_v(j)
            pltpu.make_async_remote_copy(
                src_ref=src_of(to),
                dst_ref=dst.at[me_v],
                send_sem=send_sems.at[rnd],
                recv_sem=recv_sems.at[rnd],
                device_id=(me_d, to),
                device_id_type=MESH,
            ).start()
            return carry

        lax.fori_loop(1, n_voc, one, 0)

    def wait_blocks(dst, sem, n):
        ref = dst.at[pl.ds(0, n - 1)]
        pltpu.make_async_copy(ref, ref, sem).wait()

    loads[0].wait()
    loads[1].wait()
    part = dot_t(ibuf[...], hbuf[...])
    in_part[...] = part.reshape(in_part.shape)
    in_parts[me_v] = in_part[me_v]

    pl.semaphore_wait(barrier, n_voc + n_dp - 2)
    send_v(lambda to: in_part.at[to], in_parts, 0)

    tgt = targets_ref[...] - me_v * rows
    col16 = lax.broadcasted_iota(jnp.int32, (16, tokens), 0)

    run_max = jnp.full((1, tokens), -1e30, F32)
    run_sum = jnp.zeros((8, tokens), F32)
    picked = jnp.zeros((16, tokens), BF16)
    chunk_max = []
    for c, (s, w) in enumerate(zip(starts, sizes)):
        chunk_loads[c].wait()
        group = jnp.clip((tgt - s) >> 4, -1, CHUNK // 16)
        group = jnp.broadcast_to(group, (16, tokens)).astype(F32).astype(BF16)

        n_full = w // 128
        tail = w % 128

        def scan(i, carry, s=s, count=8):
            top, sel, g = carry
            x = lbuf[pl.ds(pl.multiple_of(s + i * 128, 16), count * 16), :]
            for j in range(count):
                xj = x[16 * j : 16 * j + 16]
                top = jnp.maximum(top, xj)
                sel = jnp.where(g == BF16(j), xj, sel)
            return top, sel, g - BF16(8)

        top = jnp.full((16, tokens), -1e30, BF16)
        carry = lax.fori_loop(0, n_full, scan, (top, picked, group))
        if tail:
            carry = scan(n_full, carry, count=tail // 16)
        top, picked, _ = carry
        here = jnp.max(top.astype(F32), axis=0, keepdims=True)
        new_max = jnp.maximum(run_max, here)
        run_sum = run_sum * jnp.exp2((run_max - new_max) * LOG2E)
        run_max = new_max
        chunk_max.append(new_max)

        def exps(i, acc, s=s, count=128, new_max=new_max):
            at = pl.ds(pl.multiple_of(s + i * 128, 16), count)
            e = jnp.exp2((lbuf[at, :].astype(F32) - new_max) * LOG2E)
            ebuf[at, :] = e
            return acc + jnp.sum(e.reshape(count // 8, 8, tokens), axis=0)

        run_sum = lax.fori_loop(0, n_full, exps, run_sum)
        if tail:
            run_sum = exps(n_full, run_sum, count=tail)

        if c == 2:
            wait_blocks(in_parts, recv_sems.at[0], n_voc)
            block = jnp.sum(in_parts[...], axis=0)
            in_block[...] = block
            in_full[me_v] = block
            send_v(lambda to: in_block, in_full, 1)

    total_here = jnp.sum(run_sum, axis=0, keepdims=True)
    stat_src[0:1, :] = run_max[:, :128]
    stat_src[1:2, :] = run_max[:, 128:]
    stat_src[2:3, :] = total_here[:, :128]
    stat_src[3:4, :] = total_here[:, 128:]
    stats[me_v] = stat_src[...]
    send_v(lambda to: stat_src, stats, 2)

    loads[2].wait()
    block_of = tgt >> 8
    lane_of = tgt & 255
    pick = (lax.broadcasted_iota(jnp.int32, (256, tokens), 0) == lane_of).astype(F32).astype(BF16)

    def gather(k, acc):
        cols = pbuf[:, pl.ds(pl.multiple_of(k * 256, 256), 256)]
        found = jnp.dot(cols, pick, preferred_element_type=F32)
        return jnp.where(block_of == k, found, acc)

    n_blocks = rows // 256
    rest = rows % 256
    wanted = lax.fori_loop(0, n_blocks, gather, jnp.zeros((pbuf.shape[0], tokens), F32))
    if rest:
        found = jnp.dot(pbuf[:, n_blocks * 256 :], pick[:rest], preferred_element_type=F32)
        wanted = jnp.where(block_of == n_blocks, found, wanted)
    at_target = jnp.sum(
        jnp.where(col16 == (tgt & 15), picked.astype(F32), 0.0), axis=0, keepdims=True
    )

    wait_blocks(stats, recv_sems.at[2], n_voc)
    all_stats = stats[...]
    every_max = jnp.concatenate([all_stats[:, 0, :], all_stats[:, 1, :]], axis=1)
    every_sum = jnp.concatenate([all_stats[:, 2, :], all_stats[:, 3, :]], axis=1)
    row_max = jnp.max(every_max, axis=0, keepdims=True)
    row_total = jnp.sum(
        every_sum * jnp.exp2((every_max - row_max) * LOG2E), axis=0, keepdims=True
    )
    inverse = 1.0 / row_total
    scale = [jnp.exp2((m - row_max) * LOG2E) * inverse for m in chunk_max]

    chunk_of = tgt >> 11
    target_max = chunk_max[0]
    target_scale = scale[0]
    for c in range(1, n_chunks):
        target_max = jnp.where(chunk_of == c, chunk_max[c], target_max)
        target_scale = jnp.where(chunk_of == c, scale[c], target_scale)
    p_target = jnp.exp2((at_target - target_max) * LOG2E) * target_scale
    fix = (p_target - 1.0).astype(BF16).astype(F32) - p_target.astype(BF16).astype(F32)
    fix = jnp.where((tgt >= 0) & (tgt < rows), fix, 0.0)

    out_low = wanted * fix
    for c, (s, w) in enumerate(zip(starts, sizes)):

        def project(i, acc, s=s, c=c, count=STEP):
            first = pl.multiple_of(s + i * STEP, STEP)
            probs = (ebuf[pl.ds(first, count), :] * scale[c]).astype(BF16)
            cols = pbuf[:, pl.ds(first, count)]
            return acc + jnp.dot(cols, probs, preferred_element_type=F32)

        out_low = lax.fori_loop(0, w // STEP, project, out_low)
        if w % STEP:
            out_low = project(w // STEP, out_low, count=w % STEP)

    wait_blocks(in_full, recv_sems.at[1], n_voc)
    in_low = in_full[...].reshape(in_full.shape[0] * in_full.shape[1], tokens)
    grads = [
        dot_t(in_low[:, t : t + SEQ], out_low[:, t : t + SEQ], HIGH)
        for t in range(0, tokens, SEQ)
    ]
    eg_src[...] = jnp.concatenate(grads, axis=1).reshape(eg_src.shape)
    eg_parts[me_v] = eg_src[me_v]
    send_v(lambda to: eg_src.at[to], eg_parts, 3)

    query = query_ref[...]
    query_d = query >> 1
    query_odd = (query & 1) == 1
    lane = lax.broadcasted_iota(jnp.int32, (128, 64), 0)
    place = jnp.concatenate(
        [(lane == query_d).astype(F32), (lane == query_d + 32).astype(F32)], axis=1
    )
    half = lax.broadcasted_iota(jnp.int32, (8, 128), 1) // 64
    halves = (half == lax.broadcasted_iota(jnp.int32, (8, 128), 0)).astype(F32)

    wait_blocks(eg_parts, recv_sems.at[3], n_voc)
    mine = jnp.sum(eg_parts[...], axis=0)
    slice_src[...] = mine
    slices[pl.ds(pl.multiple_of(me_d * 8, 8), 8), :] = mine

    def share(j, carry):
        pltpu.make_async_remote_copy(
            src_ref=slice_src,
            dst_ref=slices.at[pl.ds(pl.multiple_of(me_d * 8, 8), 8)],
            send_sem=send_sems.at[4],
            recv_sem=recv_sems.at[4],
            device_id=(other_d(j), me_v),
            device_id_type=MESH,
        ).start()
        return carry

    lax.fori_loop(1, n_dp, share, 0)
    swapped = jnp.concatenate([mine[:, 64:], mine[:, :64]], axis=1)
    ref = slices.at[pl.ds(0, 8 * (n_dp - 1))]
    pltpu.make_async_copy(ref, ref, recv_sems.at[4]).wait()

    same = jnp.zeros((n_dp, 128), F32)
    cross = jnp.zeros((n_dp, 128), F32)
    square = jnp.zeros((n_dp, 128), F32)
    for i in range(8):
        rows_i = slices[pl.ds(i, n_dp, stride=8), :]
        same = same + rows_i * mine[i : i + 1]
        cross = cross + rows_i * swapped[i : i + 1]
        square = square + rows_i * rows_i
    stack = jnp.concatenate([same, cross, square, jnp.zeros((n_dp, 128), F32)], axis=0)
    partial = dot_t(halves, stack, HIGH)
    sum_src[...] = partial
    sums[me_v] = partial
    send_v(lambda to: sum_src, sums, 5)
    wait_blocks(sums, recv_sems.at[5], n_voc)
    total = jnp.sum(sums[...], axis=0)

    root = lax.rsqrt(total + 1e-6)
    root_same = jnp.concatenate(
        [root[:, 64:96], root[:, 64:96], jnp.zeros((8, 64), F32)], axis=1
    )
    scaled = total * root_same
    found = jnp.dot(scaled, place, precision=HIGH, preferred_element_type=F32)
    own = lax.broadcasted_iota(jnp.int32, (8, 128), 1) == 64 + me_d
    own_root = jnp.sum(jnp.where(own, root, 0.0), axis=1, keepdims=True)
    first = jnp.where(query_odd, found[1:2, 64:], found[0:1, :64]) * own_root[0:1]
    second = jnp.where(query_odd, found[1:2, :64], found[0:1, 64:]) * own_root[1:2]
    out_ref[...] = jnp.concatenate([first, second], axis=0)

    wait_blocks(in_part, send_sems.at[0], n_voc)
    wait_blocks(in_full, send_sems.at[1], n_voc)
    wait_blocks(stats, send_sems.at[2], n_voc)
    wait_blocks(eg_src, send_sems.at[3], n_voc)
    ref = slices.at[pl.ds(0, 8 * (n_dp - 1))]
    pltpu.make_async_copy(ref, ref, send_sems.at[4]).wait()
    wait_blocks(sums, send_sems.at[5], n_voc)


def solution(mesh):
    n_dp, n_voc = mesh.shape["dp"], mesh.shape["vocab"]

    def body(hidden_states, logits, targets, input_proj, output_proj, query_ids):
        tokens, rows = logits.shape
        feats = hidden_states.shape[1]
        r_in, r_out = input_proj.shape[1], output_proj.shape[1]
        examples = tokens // SEQ
        lanes = examples * r_out
        n_chunks = -(-rows // CHUNK)
        hbm = pl.BlockSpec(memory_space=pl.ANY)
        vmem = pl.BlockSpec(memory_space=pltpu.VMEM)
        block = r_in // n_voc
        return pl.pallas_call(
            functools.partial(kernel, n_dp, n_voc),
            out_shape=jax.ShapeDtypeStruct((examples, query_ids.shape[0]), F32),
            in_specs=[hbm, hbm, hbm, hbm, vmem, vmem],
            out_specs=vmem,
            scratch_shapes=[
                pltpu.VMEM((rows, tokens), BF16),
                pltpu.VMEM((rows, tokens), F32),
                pltpu.VMEM((r_out, rows), BF16),
                pltpu.VMEM((tokens, feats), BF16),
                pltpu.VMEM((r_in, feats), BF16),
                pltpu.VMEM((n_voc, block, tokens), F32),
                pltpu.VMEM((n_voc, block, tokens), F32),
                pltpu.VMEM((block, tokens), F32),
                pltpu.VMEM((n_voc, block, tokens), F32),
                pltpu.VMEM((8, 128), F32),
                pltpu.VMEM((n_voc, 8, 128), F32),
                pltpu.VMEM((n_voc, block, lanes), F32),
                pltpu.VMEM((n_voc, block, lanes), F32),
                pltpu.VMEM((block, lanes), F32),
                pltpu.VMEM((n_dp * block, lanes), F32),
                pltpu.VMEM((8, 128), F32),
                pltpu.VMEM((n_voc, 8, 128), F32),
                pltpu.SemaphoreType.DMA((3,)),
                pltpu.SemaphoreType.DMA((n_chunks,)),
                pltpu.SemaphoreType.DMA((6,)),
                pltpu.SemaphoreType.DMA((6,)),
            ],
            compiler_params=pltpu.CompilerParams(
                collective_id=0,
                has_side_effects=True,
                vmem_limit_bytes=56 * 1024 * 1024,
            ),
            cost_estimate=pl.CostEstimate(
                flops=2 * tokens * rows * r_out,
                bytes_accessed=2 * (tokens * rows + rows * r_out),
                transcendentals=tokens * rows,
            ),
        )(
            logits.T,
            output_proj.T,
            hidden_states,
            input_proj.T,
            targets.reshape(1, tokens),
            query_ids.reshape(1, -1),
        )

    return jax.shard_map(
        body,
        mesh=mesh,
        in_specs=(
            P("dp", "vocab"),
            P("dp", "vocab"),
            P("dp"),
            P("vocab", None),
            P("vocab", None),
            P(),
        ),
        out_specs=P("dp", None),
        check_vma=False,
    )
```

time: 221 us -> 55.8 us (0.25); the launches traced: 218 us -> 55.7 us
  waiting for transfers between devices: 139 us -> 0 us
  Pallas kernels: 0 us -> 54.5 us
  blocking collectives: 28.1 us -> 0 us
  matrix products: 16.1 us -> 0 us
  other arithmetic: 15.8 us -> 0 us
  between operations: 13.5 us -> 0.01 us
  local copies, waits for them, and re-layouts: 4.84 us -> 1.24 us
    all_gather x1 -> x0, waiting for transfers between devices: 76.3 us -> none  [body(): gathered = lax.all_gather(example_grad, 'dp', axis=0, tiled=True)]
    psum x1 -> x0, waiting for transfers between devices: 62.9 us -> none  [body(): in_low, out_low = lax.psum((in_part, out_part), 'vocab')]
    pallas_call x0 -> x1, Pallas kernels: none -> 54.5 us  [body(): pl.pallas_call(functools.partial(kernel, n_dp, n_voc), out_shape=jax.Shap...]
    dot_general x4 -> x0, matrix products: 16.1 us -> none  [the longest x1 10.8 us: body(): jnp.dot(out_grad, output_proj, preferred_element_type=jnp.float32)]
    pmax x1 -> x0, blocking collectives: 15 us -> none  [body(): row_max = lax.pmax(narrow_max, 'vocab').astype(jnp.float32)]
    psum x1 -> x0, blocking collectives: 13.1 us -> none  [body(): row_total = lax.psum(jnp.sum(exp_terms, axis=1), 'vocab')]
    reduce_sum x2 -> x0, other arithmetic: 9.11 us -> none  [the longest x1 6.5 us: body(): row_total = lax.psum(jnp.sum(exp_terms, axis=1), 'vocab')]
    reduce_max x1 -> x0, other arithmetic: 6.62 us -> none  [body(): narrow_max = jnp.max(logits, axis=1)]
  transfers between devices with their start and end apart: 2 -> 0, of which waited for: 2 -> 0; matrix products, arithmetic and copies ran while one was open for 0% -> 0% of each run, Pallas kernels for 0% -> 0%
where the time goes in v1:
time: 55.8 us; the launch traced here: 55.7 us
  Pallas kernels  54.5 us (98%)
  local copies, waits for them, and re-layouts  1.24 us (2%)
    pallas_call x1, Pallas kernels, body(): pl.pallas_call(functools.partial(kernel, n_dp, n_voc), out_shape=jax.Shap...  54.5 us
    unnamed x1, local copies, waits for them, and re-layouts  1.24 us

profile of v1, /device:TPU:1, one launch (start us, length us, event | category | flops | bytes accessed | tf_op | source)
XLA Modules:
  0.0 55.7 jit_solution(6009134028806570437)
XLA Ops:
  0.0 54.5 %shard_map.64 = f32[2,64]{1,0:T(2,128)} custom-call(bf16[16032,256]{1,0:T(8,128)(2,1)} %bitcast.5, bf16[64,16032]{1,0:T(8,128)(2,1)} %bitcast.6, bf16[256,1024]{1,0:T(8,128)(2,1)} %hidden_hbm.1, bf16[64,1024]{1,0:T(8,128)(2,1)} %bitcast.7, s32[1,256]{1,0:T(1,128)} %bitcast.8, s32[1,64]{1,0:T(1,128)} %bitcast.9), custom_call_target="tpu_custom_call" | custom-call | flops 525336576 | bytes 10260480 | tf_op jit(solution)/shard_map/pallas_call | solution.py:338
  54.5 1.2 %copy.8 = f32[2,64]{1,0:T(2,128)} copy(f32[2,64]{1,0:T(2,128)} %shard_map.64) | data formatting | bytes 1024

commit v2 on v1

v2 whole, which is shorter than its diff:
```python
import functools

import jax
import jax.numpy as jnp
from jax import lax
from jax.experimental import pallas as pl
from jax.experimental.pallas import tpu as pltpu
from jax.sharding import PartitionSpec as P

MESH = pl.DeviceIdType.MESH
F32 = jnp.float32
BF16 = jnp.bfloat16
SEQ = 128
LOG2E = 1.4426950408889634
HIGH = lax.Precision.HIGHEST
CHUNK = 2048
BLOCK = 256
LANES = 32
MSG = 24


def dot(a, b, precision=None):
    return jnp.dot(a, b, precision=precision, preferred_element_type=F32)


def dot_t(a, b, precision=None):
    return lax.dot_general(
        a, b, (((1,), (1,)), ((), ())), precision=precision, preferred_element_type=F32
    )


def ring(step, size):
    return min(step, size - step)


def kernel(
    n_x,
    n_z,
    n_y,
    logits_hbm,
    proj_hbm,
    hidden_hbm,
    inproj_hbm,
    targets_ref,
    query_ref,
    out_ref,
    lbuf,
    pbuf,
    hbuf,
    ibuf,
    in_part,
    in_parts,
    in_block,
    in_full,
    msg_src,
    msgs,
    hit_src,
    hits,
    slice_src,
    slices,
    sum_src,
    sums,
    load_sems,
    logit_sems,
    proj_sems,
    send_sems,
    recv_sems,
):
    rows, tokens = lbuf.shape
    n_dp, n_voc = n_x * n_z, n_y * 2
    me_d = lax.axis_index("dp")
    me_v = lax.axis_index("vocab")
    my_x, my_z = lax.div(me_d, n_z), lax.rem(me_d, n_z)
    my_y, my_core = lax.div(me_v, 2), lax.rem(me_v, 2)
    starts = list(range(0, rows, CHUNK))
    sizes = [min(CHUNK, rows - s) for s in starts]

    load_hidden = pltpu.make_async_copy(hidden_hbm, hbuf, load_sems.at[0])
    load_inproj = pltpu.make_async_copy(inproj_hbm, ibuf, load_sems.at[1])
    load_hidden.start()
    load_inproj.start()
    chunk_loads = []
    for c, (s, w) in enumerate(zip(starts, sizes)):
        pair = (
            pltpu.make_async_copy(
                proj_hbm.at[:, pl.ds(s, w)], pbuf.at[:, pl.ds(s, w)], proj_sems.at[c]
            ),
            pltpu.make_async_copy(
                logits_hbm.at[pl.ds(s, w)], lbuf.at[pl.ds(s, w)], logit_sems.at[c]
            ),
        )
        for copy in pair:
            copy.start()
        chunk_loads.append(pair)

    steps_v = sorted(
        [(dy, dc) for dy in range(n_y) for dc in range(2) if dy or dc],
        key=lambda s: -ring(s[0], n_y),
    )
    steps_d = sorted(
        [(dx, dz) for dx in range(n_x) for dz in range(n_z) if dx or dz],
        key=lambda s: -ring(s[0], n_x) - ring(s[1], n_z),
    )
    others_v = [
        lax.rem(my_y + dy, n_y) * 2 + lax.rem(my_core + dc, 2) for dy, dc in steps_v
    ]
    others_d = [
        lax.rem(my_x + dx, n_x) * n_z + lax.rem(my_z + dz, n_z) for dx, dz in steps_d
    ]

    barrier = pltpu.get_barrier_semaphore()
    for to in others_d:
        pl.semaphore_signal(barrier, inc=1, device_id=(to, me_v), device_id_type=MESH)
    for to in others_v:
        pl.semaphore_signal(barrier, inc=1, device_id=(me_d, to), device_id_type=MESH)

    def send_v(src_of, dst, rnd):
        for to in others_v:
            pltpu.make_async_remote_copy(
                src_ref=src_of(to),
                dst_ref=dst.at[me_v],
                send_sem=send_sems.at[rnd],
                recv_sem=recv_sems.at[rnd],
                device_id=(me_d, to),
                device_id_type=MESH,
            ).start()

    def wait_blocks(dst, sem, n):
        ref = dst.at[pl.ds(0, n - 1)]
        pltpu.make_async_copy(ref, ref, sem).wait()

    load_hidden.wait()
    load_inproj.wait()
    part = dot_t(ibuf[...], hbuf[...])
    in_part[...] = part.reshape(in_part.shape)
    in_parts[me_v] = in_part[me_v]

    pl.semaphore_wait(barrier, n_voc + n_dp - 2)
    send_v(lambda to: in_part.at[to], in_parts, 0)

    tgt = targets_ref[...] - me_v * rows
    block_of = tgt >> 8
    pick = lax.broadcasted_iota(jnp.int32, (BLOCK, tokens), 0) == (tgt & 255)
    pick = pick.astype(F32).astype(BF16)

    def wait_chunk(c):
        for copy in chunk_loads[c]:
            copy.wait()

    def largest(c):
        s, w = starts[c], sizes[c]
        x = lbuf[pl.ds(s, w), :]
        tops = [x[16 * j : 16 * j + 16] for j in range(4)]
        for j in range(4, w // 16):
            tops[j % 4] = jnp.maximum(tops[j % 4], x[16 * j : 16 * j + 16])
        top = jnp.maximum(jnp.maximum(tops[0], tops[1]), jnp.maximum(tops[2], tops[3]))
        return jnp.max(top.astype(F32), axis=0, keepdims=True)

    r_out = pbuf.shape[0]
    run_sum = jnp.zeros((LANES, tokens), F32)
    out_part = jnp.zeros((r_out, tokens), F32)
    wanted = jnp.zeros((r_out, tokens), F32)
    wait_chunk(0)
    run_max = largest(0)
    for c, (s, w) in enumerate(zip(starts, sizes)):
        last = c + 1 == len(starts)
        if not last:
            wait_chunk(c + 1)
            next_max = jnp.maximum(run_max, largest(c + 1))
        terms = jnp.exp2((lbuf[pl.ds(s, w), :].astype(F32) - run_max) * LOG2E)
        parts = [terms[i : i + LANES] for i in range(0, w, LANES)]
        while len(parts) > 1:
            pairs = [a + b for a, b in zip(parts[::2], parts[1::2])]
            parts = pairs + parts[len(pairs) * 2 :]
        run_sum = run_sum + parts[0]
        out_part = out_part + dot(pbuf[:, pl.ds(s, w)], terms.astype(BF16))
        n_blocks = w // BLOCK
        cols = [pbuf[:, pl.ds(s + BLOCK * i, BLOCK)] for i in range(n_blocks)]
        found = dot(jnp.concatenate(cols, axis=0), pick)
        for i in range(n_blocks):
            here = block_of == (s // BLOCK + i)
            wanted = jnp.where(here, found[r_out * i : r_out * (i + 1)], wanted)
        rest = w % BLOCK
        if rest:
            at = s + n_blocks * BLOCK
            found = dot(pbuf[:, pl.ds(at, rest)], pick[:rest])
            wanted = jnp.where(block_of == at // BLOCK, found, wanted)
        if not last:
            shrink = jnp.exp2((run_max - next_max) * LOG2E)
            out_part = out_part * shrink
            run_sum = run_sum * shrink
            run_max = next_max
        if c == len(starts) - 3:
            wait_blocks(in_parts, recv_sems.at[0], n_voc)
            block = jnp.sum(in_parts[...], axis=0)
            in_block[...] = block
            in_full[me_v] = block
            send_v(lambda to: in_block, in_full, 1)

    total_here = jnp.sum(run_sum, axis=0, keepdims=True)
    each = r_out // n_voc
    halves = [slice(0, 128), slice(128, 256)]
    for k, half in enumerate(halves):
        msg_src[:, each * k : each * (k + 1), :] = out_part[:, half].reshape(
            n_voc, each, 128
        )
    stat_rows = [run_max[:, halves[0]], run_max[:, halves[1]]]
    stat_rows += [total_here[:, halves[0]], total_here[:, halves[1]]]
    stat_rows = jnp.concatenate(stat_rows + [jnp.zeros((4, 128), F32)], axis=0)
    msg_src[:, 2 * each : 2 * each + 8, :] = jnp.broadcast_to(
        stat_rows[None], (n_voc, 8, 128)
    )
    send_v(lambda to: msg_src.at[to], msgs, 2)
    hit_rows = jnp.concatenate(
        [wanted[:, half].reshape(n_voc, each, 128) for half in halves], axis=1
    )
    hit_src[...] = hit_rows.astype(BF16)
    send_v(lambda to: hit_src.at[to], hits, 3)
    msgs[me_v] = msg_src[me_v]
    hits[me_v] = hit_src[me_v]

    query = query_ref[...]
    query_d = query >> 1
    query_odd = (query & 1) == 1
    lane = lax.broadcasted_iota(jnp.int32, (128, 64), 0)
    place = jnp.concatenate(
        [(lane == query_d).astype(F32), (lane == query_d + n_dp).astype(F32)], axis=1
    )
    half_of = lax.broadcasted_iota(jnp.int32, (8, 128), 1) // 64
    sum_halves = (half_of == lax.broadcasted_iota(jnp.int32, (8, 128), 0)).astype(F32)

    wait_blocks(in_full, recv_sems.at[1], n_voc)
    in_low = in_full[...].reshape(in_full.shape[0] * in_full.shape[1], tokens)
    wait_blocks(msgs, recv_sems.at[2], n_voc)
    wait_blocks(hits, recv_sems.at[3], n_voc)
    mine = []
    for k, half in enumerate(halves):
        maxima = msgs[:, 2 * each + k, :]
        row_max = jnp.max(maxima, axis=0, keepdims=True)
        weight = jnp.exp2((maxima - row_max) * LOG2E)
        row_total = jnp.sum(msgs[:, 2 * each + 2 + k, :] * weight, axis=0, keepdims=True)
        weight = weight / row_total
        out_low = jnp.zeros((each, 128), F32)
        hit = jnp.zeros((each, 128), F32)
        for v in range(n_voc):
            out_low = out_low + msgs[v, each * k : each * (k + 1), :] * weight[v : v + 1]
            hit = hit + hits[v].astype(F32)[each * k : each * (k + 1)]
        mine.append(dot_t(out_low - hit, in_low[:, half], HIGH))
    mine = jnp.concatenate(mine, axis=1)
    slice_src[...] = mine
    my_rows = pl.ds(pl.multiple_of(me_d * 8, 8), 8)
    for to in others_d:
        pltpu.make_async_remote_copy(
            src_ref=slice_src,
            dst_ref=slices.at[my_rows],
            send_sem=send_sems.at[4],
            recv_sem=recv_sems.at[4],
            device_id=(to, me_v),
            device_id_type=MESH,
        ).start()
    slices[my_rows, :] = mine
    swapped = jnp.concatenate([mine[:, 64:], mine[:, :64]], axis=1)
    ref = slices.at[pl.ds(0, 8 * (n_dp - 1))]
    pltpu.make_async_copy(ref, ref, recv_sems.at[4]).wait()

    same = jnp.zeros((n_dp, 128), F32)
    cross = jnp.zeros((n_dp, 128), F32)
    square = jnp.zeros((n_dp, 128), F32)
    for i in range(8):
        rows_i = slices[pl.ds(i, n_dp, stride=8), :]
        same = same + rows_i * mine[i : i + 1]
        cross = cross + rows_i * swapped[i : i + 1]
        square = square + rows_i * rows_i
    stack = jnp.concatenate([same, cross, square, jnp.zeros((n_dp, 128), F32)], axis=0)
    partial = dot_t(sum_halves, stack, HIGH)
    sum_src[...] = partial
    send_v(lambda to: sum_src, sums, 5)
    sums[me_v] = partial
    wait_blocks(sums, recv_sems.at[5], n_voc)
    total = jnp.sum(sums[...], axis=0)

    root = lax.rsqrt(total + 1e-6)
    root_same = jnp.concatenate(
        [root[:, 64:96], root[:, 64:96], jnp.zeros((8, 64), F32)], axis=1
    )
    found = dot(total * root_same, place, HIGH)
    own = lax.broadcasted_iota(jnp.int32, (8, 128), 1) == 2 * n_dp + me_d
    own_root = jnp.sum(jnp.where(own, root, 0.0), axis=1, keepdims=True)
    first = jnp.where(query_odd, found[1:2, 64:], found[0:1, :64]) * own_root[0:1]
    second = jnp.where(query_odd, found[1:2, :64], found[0:1, 64:]) * own_root[1:2]
    out_ref[...] = jnp.concatenate([first, second], axis=0)

    wait_blocks(in_part, send_sems.at[0], n_voc)
    wait_blocks(in_full, send_sems.at[1], n_voc)
    wait_blocks(msgs, send_sems.at[2], n_voc)
    wait_blocks(hits, send_sems.at[3], n_voc)
    ref = slices.at[pl.ds(0, 8 * (n_dp - 1))]
    pltpu.make_async_copy(ref, ref, send_sems.at[4]).wait()
    wait_blocks(sums, send_sems.at[5], n_voc)


def solution(mesh):
    n_dp, n_voc = mesh.shape["dp"], mesh.shape["vocab"]
    n_x, n_z, n_y = 4, 8, 4

    def body(hidden_states, logits, targets, input_proj, output_proj, query_ids):
        tokens, rows = logits.shape
        feats = hidden_states.shape[1]
        r_in, r_out = input_proj.shape[1], output_proj.shape[1]
        examples = tokens // SEQ
        lanes = examples * r_in
        n_chunks = -(-rows // CHUNK)
        hbm = pl.BlockSpec(memory_space=pl.ANY)
        vmem = pl.BlockSpec(memory_space=pltpu.VMEM)
        in_block = r_in // n_voc
        out_block = r_out // n_voc
        return pl.pallas_call(
            functools.partial(kernel, n_x, n_z, n_y),
            out_shape=jax.ShapeDtypeStruct((examples, query_ids.shape[0]), F32),
            in_specs=[hbm, hbm, hbm, hbm, vmem, vmem],
            out_specs=vmem,
            scratch_shapes=[
                pltpu.VMEM((rows, tokens), BF16),
                pltpu.VMEM((r_out, rows), BF16),
                pltpu.VMEM((tokens, feats), BF16),
                pltpu.VMEM((r_in, feats), BF16),
                pltpu.VMEM((n_voc, in_block, tokens), F32),
                pltpu.VMEM((n_voc, in_block, tokens), F32),
                pltpu.VMEM((in_block, tokens), F32),
                pltpu.VMEM((n_voc, in_block, tokens), F32),
                pltpu.VMEM((n_voc, MSG, 128), F32),
                pltpu.VMEM((n_voc, MSG, 128), F32),
                pltpu.VMEM((n_voc, 2 * out_block, 128), BF16),
                pltpu.VMEM((n_voc, 2 * out_block, 128), BF16),
                pltpu.VMEM((out_block, lanes), F32),
                pltpu.VMEM((n_dp * out_block, lanes), F32),
                pltpu.VMEM((8, 128), F32),
                pltpu.VMEM((n_voc, 8, 128), F32),
                pltpu.SemaphoreType.DMA((2,)),
                pltpu.SemaphoreType.DMA((n_chunks,)),
                pltpu.SemaphoreType.DMA((n_chunks,)),
                pltpu.SemaphoreType.DMA((6,)),
                pltpu.SemaphoreType.DMA((6,)),
            ],
            compiler_params=pltpu.CompilerParams(
                collective_id=0,
                has_side_effects=True,
                vmem_limit_bytes=56 * 1024 * 1024,
            ),
            cost_estimate=pl.CostEstimate(
                flops=2 * tokens * rows * r_out,
                bytes_accessed=2 * (tokens * rows + rows * r_out),
                transcendentals=tokens * rows,
            ),
        )(
            logits.T,
            output_proj.T,
            hidden_states,
            input_proj.T,
            targets.reshape(1, tokens),
            query_ids.reshape(1, -1),
        )

    return jax.shard_map(
        body,
        mesh=mesh,
        in_specs=(
            P("dp", "vocab"),
            P("dp", "vocab"),
            P("dp"),
            P("vocab", None),
            P("vocab", None),
            P(),
        ),
        out_specs=P("dp", None),
        check_vma=False,
    )
```

time: 55.8 us -> 34 us (0.61)
  Pallas kernels: 54.5 us -> 32.7 us
    pallas_call x1, Pallas kernels: 54.5 us -> 32.7 us  [body(): pl.pallas_call(functools.partial(kernel, n_x, n_z, n_y), out_shape=jax.Sh...]
where the time goes in v2:
time: 34 us; the launch traced here: 33.9 us
  Pallas kernels  32.7 us (96%)
  local copies, waits for them, and re-layouts  1.24 us (4%)
    pallas_call x1, Pallas kernels, body(): pl.pallas_call(functools.partial(kernel, n_x, n_z, n_y), out_shape=jax.Sh...  32.7 us
    unnamed x1, local copies, waits for them, and re-layouts  1.24 us

profile of v2, /device:TPU:1, one launch (start us, length us, event | category | flops | bytes accessed | tf_op | source)
XLA Modules:
  0.0 33.9 jit_solution(14889154138805135070)
XLA Ops:
  0.0 32.7 %shard_map.64 = f32[2,64]{1,0:T(2,128)} custom-call(bf16[16032,256]{1,0:T(8,128)(2,1)} %bitcast.5, bf16[64,16032]{1,0:T(8,128)(2,1)} %bitcast.6, bf16[256,1024]{1,0:T(8,128)(2,1)} %hidden_hbm.1, bf16[64,1024]{1,0:T(8,128)(2,1)} %bitcast.7, s32[1,256]{1,0:T(1,128)} %bitcast.8, s32[1,64]{1,0:T(1,128)} %bitcast.9), custom_call_target="tpu_custom_call" | custom-call | flops 525336576 | bytes 10260480 | tf_op jit(solution)/shard_map/pallas_call | solution.py:317
  32.7 1.2 %copy.8 = f32[2,64]{1,0:T(2,128)} copy(f32[2,64]{1,0:T(2,128)} %shard_map.64) | data formatting | bytes 1024

commit v3 on v2

v3 whole, which is shorter than its diff:
```python
import functools

import jax
import jax.numpy as jnp
from jax import lax
from jax.experimental import pallas as pl
from jax.experimental.pallas import tpu as pltpu
from jax.sharding import PartitionSpec as P

MESH = pl.DeviceIdType.MESH
F32 = jnp.float32
BF16 = jnp.bfloat16
SEQ = 128
LOG2E = 1.4426950408889634
HIGH = lax.Precision.HIGHEST
BLOCK = 256
SIZES = (2048, 2048, 2048, 2048, 2048, 2048, 2048, 1696)
INPUTS = 1
GREET = 1
SHARE = 3
HITS = 3
MSG = 40


def dot(a, b, precision=None):
    return jnp.dot(a, b, precision=precision, preferred_element_type=F32)


def dot_t(a, b, precision=None):
    return lax.dot_general(
        a, b, (((1,), (1,)), ((), ())), precision=precision, preferred_element_type=F32
    )


def ring(step, size):
    return min(step, size - step)


def kernel(
    n_x,
    n_z,
    n_y,
    logits_hbm,
    proj_hbm,
    hidden_hbm,
    inproj_hbm,
    targets_hbm,
    query_hbm,
    out_ref,
    targets_ref,
    query_ref,
    lbuf,
    pbuf,
    hbuf,
    ibuf,
    in_part,
    in_pair,
    in_sum,
    in_sums,
    msg_src,
    msgs,
    hit_src,
    hits,
    slice_src,
    slices,
    sum_src,
    sums,
    load_sems,
    logit_sems,
    proj_sems,
    send_sems,
    recv_sems,
):
    rows, tokens = lbuf.shape
    n_dp, n_voc = n_x * n_z, n_y * 2
    me_d = lax.axis_index("dp")
    me_v = lax.axis_index("vocab")
    my_x, my_z = lax.div(me_d, n_z), lax.rem(me_d, n_z)
    my_y, my_core = lax.div(me_v, 2), lax.rem(me_v, 2)
    sizes = SIZES
    starts = [sum(sizes[:c]) for c in range(len(sizes))]
    n_chunks = len(sizes)

    load_hidden = pltpu.make_async_copy(hidden_hbm, hbuf, load_sems.at[0])
    load_inproj = pltpu.make_async_copy(inproj_hbm, ibuf, load_sems.at[1])
    r_out = proj_hbm.shape[0]
    proj_loads = [
        pltpu.make_async_copy(
            proj_hbm.at[:, pl.ds(s, w)],
            pbuf.at[pl.ds(0, r_out), pl.ds(s, w)],
            proj_sems.at[c],
        )
        for c, (s, w) in enumerate(zip(starts, sizes))
    ]
    logit_loads = [
        pltpu.make_async_copy(
            logits_hbm.at[pl.ds(s, w)], lbuf.at[pl.ds(s, w)], logit_sems.at[c]
        )
        for c, (s, w) in enumerate(zip(starts, sizes))
    ]
    load_targets = pltpu.make_async_copy(targets_hbm, targets_ref, load_sems.at[2])
    load_query = pltpu.make_async_copy(query_hbm, query_ref, load_sems.at[3])
    load_targets.start()
    for c in range(n_chunks):
        for copy in proj_loads[2 * c : 2 * c + 2]:
            copy.start()
        logit_loads[c].start()
        if c == 0:
            load_hidden.start()
            load_inproj.start()
            load_query.start()

    steps_v = sorted(
        [(dy, dc) for dy in range(n_y) for dc in range(2) if dy or dc],
        key=lambda s: -ring(s[0], n_y),
    )
    steps_d = sorted(
        [(dx, dz) for dx in range(n_x) for dz in range(n_z) if dx or dz],
        key=lambda s: -ring(s[0], n_x) - ring(s[1], n_z),
    )
    others_v = [
        lax.rem(my_y + dy, n_y) * 2 + lax.rem(my_core + dc, 2) for dy, dc in steps_v
    ]
    others_d = [
        lax.rem(my_x + dx, n_x) * n_z + lax.rem(my_z + dz, n_z) for dx, dz in steps_d
    ]

    barrier = pltpu.get_barrier_semaphore()
    for to in others_d:
        pl.semaphore_signal(barrier, inc=1, device_id=(to, me_v), device_id_type=MESH)
    for to in others_v:
        pl.semaphore_signal(barrier, inc=1, device_id=(me_d, to), device_id_type=MESH)

    def remote(src_ref, dst_ref, rnd, to):
        return pltpu.make_async_remote_copy(
            src_ref=src_ref,
            dst_ref=dst_ref,
            send_sem=send_sems.at[rnd],
            recv_sem=recv_sems.at[rnd],
            device_id=to,
            device_id_type=MESH,
        )

    def send_v(src_of, dst, rnd):
        for to in others_v:
            remote(src_of(lax.div(to, 2)), dst.at[me_v], rnd, (me_d, to)).start()

    def wait_blocks(dst, sem, n):
        ref = dst.at[pl.ds(0, n - 1)]
        pltpu.make_async_copy(ref, ref, sem).wait()

    pbuf[r_out:, :] = jnp.ones((pbuf.shape[0] - r_out, rows), BF16)

    def project_inputs():
        load_hidden.wait()
        load_inproj.wait()
        in_part[...] = dot_t(ibuf[...], hbuf[...]).reshape(in_part.shape)

    other_core = 1 - my_core
    swap_halves = remote(
        in_part.at[other_core], in_pair, 0, (me_d, my_y * 2 + other_core)
    )

    def greet():
        pl.semaphore_wait(barrier, n_voc + n_dp - 2)
        swap_halves.start()

    def share_inputs():
        swap_halves.wait_recv()
        both = in_part[my_core] + in_pair[...]
        in_sum[...] = both
        in_sums[my_y] = both
        for dy in (n_y // 2, 1, n_y - 1):
            to = lax.rem(my_y + dy, n_y) * 2 + my_core
            remote(in_sum, in_sums.at[my_y], 1, (me_d, to)).start()

    load_targets.wait()
    tgt = targets_ref[...] - me_v * rows
    block_of = tgt >> 8
    pick = lax.broadcasted_iota(jnp.int32, (BLOCK, tokens), 0) == (tgt & 255)
    pick = pick.astype(F32).astype(BF16)

    def largest(c):
        s, w = starts[c], sizes[c]
        x = lbuf[pl.ds(s, w), :]
        tops = [x[16 * j : 16 * j + 16] for j in range(4)]
        for j in range(4, w // 16):
            tops[j % 4] = jnp.maximum(tops[j % 4], x[16 * j : 16 * j + 16])
        top = jnp.maximum(jnp.maximum(tops[0], tops[1]), jnp.maximum(tops[2], tops[3]))
        return jnp.max(top.astype(F32), axis=0, keepdims=True)

    def gather(c, wanted):
        s, w = starts[c], sizes[c]
        n_blocks = w // BLOCK
        cols = [pbuf[:r_out, pl.ds(s + BLOCK * i, BLOCK)] for i in range(n_blocks)]
        found = dot(jnp.concatenate(cols, axis=0), pick)
        for i in range(n_blocks):
            here = block_of == (s // BLOCK + i)
            wanted = jnp.where(here, found[r_out * i : r_out * (i + 1)], wanted)
        rest = w % BLOCK
        if rest:
            at = s + n_blocks * BLOCK
            found = dot(pbuf[:r_out, pl.ds(at, rest)], pick[:rest])
            wanted = jnp.where(block_of == at // BLOCK, found, wanted)
        return wanted

    out_part = jnp.zeros((pbuf.shape[0], tokens), F32)
    wanted = jnp.zeros((r_out, tokens), F32)
    each = r_out // n_y
    halves = [slice(0, 128), slice(128, 256)]
    logit_loads[0].wait()
    run_max = largest(0)
    for c, (s, w) in enumerate(zip(starts, sizes)):
        last = c + 1 == n_chunks
        for copy in proj_loads[2 * c : 2 * c + 2]:
            copy.wait()
        if not last:
            logit_loads[c + 1].wait()
            next_max = jnp.maximum(run_max, largest(c + 1))
        terms = jnp.exp2((lbuf[pl.ds(s, w), :].astype(F32) - run_max) * LOG2E)
        out_part = out_part + dot(pbuf[:, pl.ds(s, w)], terms.astype(BF16))
        for piece in range(2 * c, min(2 * c + 2, n_chunks)):
            wanted = gather(piece, wanted)
        if not last:
            out_part = out_part * jnp.exp2((run_max - next_max) * LOG2E)
            run_max = next_max
        if c == INPUTS:
            project_inputs()
        if c == GREET:
            greet()
        if c == HITS:
            for k, half in enumerate(halves):
                hit_src[:, each * k : each * (k + 1), :] = (
                    wanted[:, half].reshape(n_y, each, 128).astype(BF16)
                )
            send_v(lambda to: hit_src.at[to], hits, 3)
            hits[me_v] = hit_src[my_y]
        if c == SHARE:
            share_inputs()

    for k, half in enumerate(halves):
        msg_src[:, each * k : each * (k + 1), :] = out_part[:r_out, half].reshape(
            n_y, each, 128
        )
    total_here = out_part[r_out : r_out + 1]
    stat_rows = [run_max[:, halves[0]], run_max[:, halves[1]]]
    stat_rows += [total_here[:, halves[0]], total_here[:, halves[1]]]
    stat_rows = jnp.concatenate(stat_rows + [jnp.zeros((4, 128), F32)], axis=0)
    msg_src[:, 2 * each : 2 * each + 8, :] = jnp.broadcast_to(
        stat_rows[None], (n_y, 8, 128)
    )
    send_v(lambda to: msg_src.at[to], msgs, 2)
    msgs[me_v] = msg_src[my_y]

    load_query.wait()
    query = query_ref[...]
    query_d = query >> 1
    query_odd = (query & 1) == 1
    lane = lax.broadcasted_iota(jnp.int32, (128, 64), 0)
    place = jnp.concatenate(
        [(lane == query_d).astype(F32), (lane == query_d + n_dp).astype(F32)], axis=1
    )
    half_of = (lax.broadcasted_iota(jnp.int32, (8, 128), 1) >> 5) & 1
    sum_halves = (half_of == lax.broadcasted_iota(jnp.int32, (8, 128), 0)).astype(F32)

    wait_blocks(in_sums, recv_sems.at[1], n_y)
    in_low = jnp.sum(in_sums[...], axis=0)
    wait_blocks(msgs, recv_sems.at[2], n_voc)
    wait_blocks(hits, recv_sems.at[3], n_voc)
    mine = []
    for k, half in enumerate(halves):
        maxima = msgs[:, 2 * each + k, :]
        row_max = jnp.max(maxima, axis=0, keepdims=True)
        weight = jnp.exp2((maxima - row_max) * LOG2E)
        row_total = jnp.sum(msgs[:, 2 * each + 2 + k, :] * weight, axis=0, keepdims=True)
        weight = weight / row_total
        out_low = jnp.zeros((each, 128), F32)
        hit = jnp.zeros((each, 128), F32)
        for v in range(n_voc):
            out_low = out_low + msgs[v, each * k : each * (k + 1), :] * weight[v : v + 1]
            hit = hit + hits[v].astype(F32)[each * k : each * (k + 1)]
        mine.append(dot_t(out_low - hit, in_low[:, half], HIGH))
    top, bottom = slice(0, 8), slice(8, 16)
    one, two = mine
    mine = jnp.concatenate([one[top], two[top], one[bottom], two[bottom]], axis=1)
    swapped = jnp.concatenate([two[top], one[top], two[bottom], one[bottom]], axis=1)
    slice_src[...] = mine
    my_rows = pl.ds(pl.multiple_of(me_d * 8, 8), 8)
    for to in others_d:
        remote(slice_src, slices.at[my_rows], 4, (to, me_v)).start()
    slices[my_rows, :] = mine
    ref = slices.at[pl.ds(0, 8 * (n_dp - 1))]
    pltpu.make_async_copy(ref, ref, recv_sems.at[4]).wait()

    same = jnp.zeros((n_dp, 128), F32)
    cross = jnp.zeros((n_dp, 128), F32)
    square = jnp.zeros((n_dp, 128), F32)
    for i in range(8):
        rows_i = slices[pl.ds(i, n_dp, stride=8), :]
        same = same + rows_i * mine[i : i + 1]
        cross = cross + rows_i * swapped[i : i + 1]
        square = square + rows_i * rows_i
    stack = jnp.concatenate([same, cross, square, jnp.zeros((n_dp, 128), F32)], axis=0)
    partial = dot_t(sum_halves, stack, HIGH)
    sum_src[...] = partial
    for to in others_v:
        remote(sum_src, sums.at[me_v], 5, (me_d, to)).start()
    sums[me_v] = partial
    wait_blocks(sums, recv_sems.at[5], n_voc)
    total = jnp.sum(sums[...], axis=0)

    root = lax.rsqrt(total + 1e-6)
    root_same = jnp.concatenate(
        [root[:, 64:96], root[:, 64:96], jnp.zeros((8, 64), F32)], axis=1
    )
    found = dot(total * root_same, place, HIGH)
    own = lax.broadcasted_iota(jnp.int32, (8, 128), 1) == 2 * n_dp + me_d
    own_root = jnp.sum(jnp.where(own, root, 0.0), axis=1, keepdims=True)
    first = jnp.where(query_odd, found[1:2, 64:], found[0:1, :64]) * own_root[0:1]
    second = jnp.where(query_odd, found[1:2, :64], found[0:1, 64:]) * own_root[1:2]
    out_ref[...] = jnp.concatenate([first, second], axis=0)

    swap_halves.wait_send()
    wait_blocks(in_sums, send_sems.at[1], n_y)
    wait_blocks(msgs, send_sems.at[2], n_voc)
    wait_blocks(hits, send_sems.at[3], n_voc)
    ref = slices.at[pl.ds(0, 8 * (n_dp - 1))]
    pltpu.make_async_copy(ref, ref, send_sems.at[4]).wait()
    wait_blocks(sums, send_sems.at[5], n_voc)


def solution(mesh):
    n_dp, n_voc = mesh.shape["dp"], mesh.shape["vocab"]
    n_x, n_z, n_y = 4, 8, 4

    def body(hidden_states, logits, targets, input_proj, output_proj, query_ids):
        tokens, rows = logits.shape
        feats = hidden_states.shape[1]
        r_in, r_out = input_proj.shape[1], output_proj.shape[1]
        examples = tokens // SEQ
        lanes = 128
        n_chunks = len(SIZES)
        hbm = pl.BlockSpec(memory_space=pl.ANY)
        vmem = pl.BlockSpec(memory_space=pltpu.VMEM)
        half = r_in // 2
        out_block = r_out // n_y
        return pl.pallas_call(
            functools.partial(kernel, n_x, n_z, n_y),
            out_shape=jax.ShapeDtypeStruct((examples, query_ids.shape[0]), F32),
            in_specs=[hbm] * 6,
            out_specs=vmem,
            scratch_shapes=[
                pltpu.VMEM((1, tokens), jnp.int32),
                pltpu.VMEM((1, query_ids.shape[0]), jnp.int32),
                pltpu.VMEM((rows, tokens), BF16),
                pltpu.VMEM((r_out + 16, rows), BF16),
                pltpu.VMEM((tokens, feats), BF16),
                pltpu.VMEM((r_in, feats), BF16),
                pltpu.VMEM((2, half, tokens), F32),
                pltpu.VMEM((half, tokens), F32),
                pltpu.VMEM((half, tokens), F32),
                pltpu.VMEM((n_y, half, tokens), F32),
                pltpu.VMEM((n_y, MSG, 128), F32),
                pltpu.VMEM((n_voc, MSG, 128), F32),
                pltpu.VMEM((n_y, 2 * out_block, 128), BF16),
                pltpu.VMEM((n_voc, 2 * out_block, 128), BF16),
                pltpu.VMEM((8, lanes), F32),
                pltpu.VMEM((n_dp * 8, lanes), F32),
                pltpu.VMEM((8, 128), F32),
                pltpu.VMEM((n_voc, 8, 128), F32),
                pltpu.SemaphoreType.DMA((4,)),
                pltpu.SemaphoreType.DMA((n_chunks,)),
                pltpu.SemaphoreType.DMA((n_chunks,)),
                pltpu.SemaphoreType.DMA((6,)),
                pltpu.SemaphoreType.DMA((6,)),
            ],
            compiler_params=pltpu.CompilerParams(
                collective_id=0,
                has_side_effects=True,
                vmem_limit_bytes=56 * 1024 * 1024,
            ),
            cost_estimate=pl.CostEstimate(
                flops=2 * tokens * rows * r_out,
                bytes_accessed=2 * (tokens * rows + rows * r_out),
                transcendentals=tokens * rows,
            ),
        )(
            logits.T,
            output_proj.T,
            hidden_states,
            input_proj.T,
            targets.reshape(1, tokens),
            query_ids.reshape(1, -1),
        )

    return jax.shard_map(
        body,
        mesh=mesh,
        in_specs=(
            P("dp", "vocab"),
            P("dp", "vocab"),
            P("dp"),
            P("vocab", None),
            P("vocab", None),
            P(),
        ),
        out_specs=P("dp", None),
        check_vma=False,
    )
```

time: 34 us -> 31.7 us (0.932)
  Pallas kernels: 32.7 us -> 30.3 us
    pallas_call x1, Pallas kernels: 32.7 us -> 30.3 us  [body(): pl.pallas_call(functools.partial(kernel, n_x, n_z, n_y), out_shape=jax.Sh...]
where the time goes in v3:
time: 31.7 us; the launch traced here: 31.6 us
  Pallas kernels  30.3 us (96%)
  local copies, waits for them, and re-layouts  1.24 us (4%)
    pallas_call x1, Pallas kernels, body(): pl.pallas_call(functools.partial(kernel, n_x, n_z, n_y), out_shape=jax.Sh...  30.3 us
    unnamed x1, local copies, waits for them, and re-layouts  1.24 us

profile of v3, /device:TPU:1, one launch (start us, length us, event | category | flops | bytes accessed | tf_op | source)
XLA Modules:
  0.0 31.6 jit_solution(11976473898072801184)
XLA Ops:
  0.0 30.3 %shard_map.64 = f32[2,64]{1,0:T(2,128)} custom-call(bf16[16032,256]{1,0:T(8,128)(2,1)} %bitcast.5, bf16[64,16032]{1,0:T(8,128)(2,1)} %bitcast.6, bf16[256,1024]{1,0:T(8,128)(2,1)} %hidden_hbm.1, bf16[64,1024]{1,0:T(8,128)(2,1)} %bitcast.7, s32[1,256]{1,0:T(1,128)} %bitcast.8, s32[1,64]{1,0:T(1,128)} %bitcast.9), custom_call_target="tpu_custom_call" | custom-call | flops 525336576 | bytes 10260480 | tf_op jit(solution)/shard_map/pallas_call | solution.py:347
  30.3 1.2 %copy.8 = f32[2,64]{1,0:T(2,128)} copy(f32[2,64]{1,0:T(2,128)} %shard_map.64) | data formatting | bytes 1024

commit v4 on v3

--- a/solution.py
+++ b/solution.py
@@ -265,8 +265,9 @@
 
     wait_blocks(in_sums, recv_sems.at[1], n_y)
     in_low = jnp.sum(in_sums[...], axis=0)
+    wait_blocks(hits, recv_sems.at[3], n_voc)
+    hit_sum = jnp.sum(hits[...].astype(F32), axis=0)
     wait_blocks(msgs, recv_sems.at[2], n_voc)
-    wait_blocks(hits, recv_sems.at[3], n_voc)
     mine = []
     for k, half in enumerate(halves):
         maxima = msgs[:, 2 * each + k, :]
@@ -275,10 +276,9 @@
         row_total = jnp.sum(msgs[:, 2 * each + 2 + k, :] * weight, axis=0, keepdims=True)
         weight = weight / row_total
         out_low = jnp.zeros((each, 128), F32)
-        hit = jnp.zeros((each, 128), F32)
+        hit = hit_sum[each * k : each * (k + 1)]
         for v in range(n_voc):
             out_low = out_low + msgs[v, each * k : each * (k + 1), :] * weight[v : v + 1]
-            hit = hit + hits[v].astype(F32)[each * k : each * (k + 1)]
         mine.append(dot_t(out_low - hit, in_low[:, half], HIGH))
     top, bottom = slice(0, 8), slice(8, 16)
     one, two = mine
@@ -304,10 +304,12 @@
     partial = dot_t(sum_halves, stack, HIGH)
     sum_src[...] = partial
     for to in others_v:
-        remote(sum_src, sums.at[me_v], 5, (me_d, to)).start()
+        remote(sum_src.at[pl.ds(0, 2)], sums.at[me_v, pl.ds(0, 2)], 5, (me_d, to)).start()
     sums[me_v] = partial
-    wait_blocks(sums, recv_sems.at[5], n_voc)
-    total = jnp.sum(sums[...], axis=0)
+    ref = sums.at[pl.ds(0, n_voc - 1), pl.ds(0, 2)]
+    pltpu.make_async_copy(ref, ref, recv_sems.at[5]).wait()
+    total = jnp.sum(sums[:, 0:2, :], axis=0)
+    total = jnp.concatenate([total, jnp.zeros((6, 128), F32)], axis=0)
 
     root = lax.rsqrt(total + 1e-6)
     root_same = jnp.concatenate(
@@ -326,7 +328,8 @@
     wait_blocks(hits, send_sems.at[3], n_voc)
     ref = slices.at[pl.ds(0, 8 * (n_dp - 1))]
     pltpu.make_async_copy(ref, ref, send_sems.at[4]).wait()
-    wait_blocks(sums, send_sems.at[5], n_voc)
+    ref = sums.at[pl.ds(0, n_voc - 1), pl.ds(0, 2)]
+    pltpu.make_async_copy(ref, ref, send_sems.at[5]).wait()
 
 
 def solution(mesh):

time: 31.7 us -> 31.6 us (level)
  no operation moved by 1% of the time
where the time goes in v4:
time: 31.6 us; the launch traced here: 31.5 us
  Pallas kernels  30.3 us (96%)
  local copies, waits for them, and re-layouts  1.24 us (4%)
    pallas_call x1, Pallas kernels, body(): pl.pallas_call(functools.partial(kernel, n_x, n_z, n_y), out_shape=jax.Sh...  30.3 us
    unnamed x1, local copies, waits for them, and re-layouts  1.24 us

profile of v4, /device:TPU:1, one launch (start us, length us, event | category | flops | bytes accessed | tf_op | source)
XLA Modules:
  0.0 31.5 jit_solution(5984127070748018286)
XLA Ops:
  0.0 30.3 %shard_map.64 = f32[2,64]{1,0:T(2,128)} custom-call(bf16[16032,256]{1,0:T(8,128)(2,1)} %bitcast.5, bf16[64,16032]{1,0:T(8,128)(2,1)} %bitcast.6, bf16[256,1024]{1,0:T(8,128)(2,1)} %hidden_hbm.1, bf16[64,1024]{1,0:T(8,128)(2,1)} %bitcast.7, s32[1,256]{1,0:T(1,128)} %bitcast.8, s32[1,64]{1,0:T(1,128)} %bitcast.9), custom_call_target="tpu_custom_call" | custom-call | flops 525336576 | bytes 10260480 | tf_op jit(solution)/shard_map/pallas_call | solution.py:350
  30.3 1.2 %copy.8 = f32[2,64]{1,0:T(2,128)} copy(f32[2,64]{1,0:T(2,128)} %shard_map.64) | data formatting | bytes 1024
